TPU v7x, 32 devices: a whole 2x2x4 slice. The times are simulated.
32 devices in a mesh: groups: 2 (over y), tm: 4 (over z), heads: 4 (over x, core).
Axes of the slice: x: 2, y: 2, z: 4, core: 2. Of those that a mesh axis runs over, the one named last changes fastest.
Arguments:
- wave_feats: bfloat16 [5120, 512], P(('groups', 'tm')), parts along dimension 0, may hold values from -6 to 6
- conv_weight: bfloat16 [2, 512, 512], P(None, None, 'heads'), may hold values from -0.1875 to 0.1875
- proj_weight: bfloat16 [512, 1280], P('heads'), may hold values from -0.25 to 0.25
- ln_gain: float32 [1280], replicated, may hold values from 0.1 to 1.9
- qkv_weight: bfloat16 [1280, 3, 1280], P(None, None, 'heads'), may hold values from -1 to 1
- out_weight: bfloat16 [1280, 1280], P(None, 'heads'), may hold values from -0.15625 to 0.15625
- depth_weight: float32 [31, 1280], P(None, 'heads'), may hold values from -1 to 1
- depth_scale: float32 [1280], P('heads'), may hold values from 0.5 to 2
- depth_shift: float32 [1280], P('heads'), may hold values from -3 to 3
- seg_ids: int32 [2560], P('groups'), parts along dimension 0, may hold values from 0 to 7, never falling along the last dimension, each value on 1 to 320 neighbouring positions
- phrase_ids: int32 [8, 512], P('groups'), parts along dimension 0, may hold values from 0 to 8191, as said below
- counts: int32 [8], P('groups'), parts along dimension 0, may hold values from 1 to 512, 1024 in all
- phrase_store: bfloat16 [8192, 2, 1280], P('tm', None, 'heads'), may hold values from -9 to 9
Outputs:
- scored: bfloat16 [2560, 1280], P(('groups', 'tm'), 'heads'), parts along dimension 0
There are 2 independent parts, one for each index of `groups`. A program takes and returns all parts, laid end to end along the dimension named above; an argument that names none is the same for every part. Nothing has to cross between parts.
Inputs may be any that keep to these rules, and one draw needn't show every extreme that they name: `phrase_ids`: each segment's list names phrases of exactly 2 owners, exactly 256 slots for each of them, the owner of phrase p being p // 2048; ids may repeat.
All inputs are finite; a program needn't handle non-finite values.
Results may differ from a plain program's by a relative error of at most 0.0085.
The roundings to bfloat16 on the way count: a program that leaves them out, or rounds other values in their place, can miss the bound.
Values may be sent and summed in bfloat16 or wider, within the bound.
A program may use at most 64 MiB of HBM per device.

v0:
```python
import math

import jax
import jax.numpy as jnp
from jax import lax
from jax.sharding import PartitionSpec as P

HEAD_DIM = 64


def extended(cells, sides, width):
    for axis, dim in sides:
        count = lax.axis_size(axis)
        ends = count - 1
        head = lax.slice_in_dim(cells, 0, width, axis=dim)
        tail = lax.slice_in_dim(cells, cells.shape[dim] - width, cells.shape[dim], axis=dim)
        cells = jnp.concatenate(
            [
                lax.ppermute(tail, axis, [(i, (i + 1) % count) for i in range(ends)]),
                cells,
                lax.ppermute(head, axis, [((i + 1) % count, i) for i in range(ends)]),
            ],
            axis=dim,
        )
    return cells


def layer_norm(values, gain):
    centre = jnp.mean(values, axis=-1, keepdims=True)
    centred = values - centre
    variance = jnp.mean(centred * centred, axis=-1, keepdims=True)
    return centred * lax.rsqrt(variance + 1e-05) * gain


def attend(queries, keys_all, values_all, allowed):
    query_heads = queries.reshape(queries.shape[0], -1, HEAD_DIM)
    key_heads = keys_all.reshape(keys_all.shape[0], -1, HEAD_DIM)
    value_heads = values_all.reshape(values_all.shape[0], -1, HEAD_DIM)
    scores = jnp.einsum(
        "qhd,khd->hqk", query_heads, key_heads, preferred_element_type=jnp.float32
    ) / math.sqrt(HEAD_DIM)
    scores = jnp.where(allowed[None], scores, -1e30)
    highest = jnp.max(scores, axis=-1, keepdims=True)
    raised = jnp.where(allowed[None], jnp.exp(scores - highest), 0.0)
    weights = (raised / jnp.sum(raised, axis=-1, keepdims=True)).astype(jnp.bfloat16)
    output = jnp.einsum("hqk,khd->qhd", weights, value_heads, preferred_element_type=jnp.float32)
    return output.reshape(queries.shape[0], -1).astype(jnp.bfloat16)


def body(
    wave_feats,
    conv_weight,
    proj_weight,
    ln_gain,
    qkv_weight,
    out_weight,
    depth_weight,
    depth_scale,
    depth_shift,
    seg_ids,
    phrase_ids,
    counts,
    phrase_store,
):
    seg_rows = wave_feats.shape[0] // 2
    channels = wave_feats.shape[1]
    head_cols = qkv_weight.shape[2]
    frame_pairs = wave_feats.reshape(seg_rows, 2 * channels)
    conv_out = jax.nn.gelu(
        jnp.dot(
            frame_pairs, conv_weight.reshape(2 * channels, -1), preferred_element_type=jnp.float32
        ),
        approximate=False,
    ).astype(jnp.bfloat16)
    partial_sum = jnp.dot(conv_out, proj_weight, preferred_element_type=jnp.float32)
    hidden = lax.psum(partial_sum, "heads").astype(jnp.bfloat16)
    normed = layer_norm(hidden.astype(jnp.float32), ln_gain).astype(jnp.bfloat16)
    proj_qkv = jnp.einsum(
        "fd,djc->fjc", normed, qkv_weight, preferred_element_type=jnp.float32
    ).astype(jnp.bfloat16)
    window_kv = extended(proj_qkv[:, 1:3], (("tm", 0),), seg_rows)
    segment = lax.axis_index("tm")
    segments = lax.axis_size("tm")
    padded_ids = jnp.pad(seg_ids, (seg_rows, seg_rows), constant_values=-1)
    window_ids = lax.dynamic_slice_in_dim(padded_ids, segment * seg_rows, 3 * seg_rows, 0)
    own_ids = lax.dynamic_slice_in_dim(seg_ids, segment * seg_rows, seg_rows, 0)
    slots = phrase_ids.shape[1]
    capacity = 2 * slots // segments
    store_rows = phrase_store.shape[0]
    owners = phrase_ids // store_rows
    local_rows = phrase_ids % store_rows
    held_here = owners == segment
    held_rank = jnp.cumsum(held_here.astype(jnp.int32), axis=1) - 1
    target_slot = jnp.where(held_here, held_rank, capacity)
    source_row = jnp.broadcast_to(jnp.arange(segments, dtype=jnp.int32)[:, None], phrase_ids.shape)
    requests = (
        jnp.zeros((segments, capacity), jnp.int32)
        .at[source_row, target_slot]
        .set(local_rows, mode="drop")
    )
    outgoing = phrase_store[requests]
    incoming = lax.all_to_all(outgoing, "tm", split_axis=0, concat_axis=0, tiled=True)
    my_list = lax.dynamic_index_in_dim(phrase_ids, segment, 0, keepdims=False)
    my_owner = my_list // store_rows
    shared_owner = my_owner[:, None] == my_owner[None, :]
    slot_index = jnp.arange(slots, dtype=jnp.int32)
    earlier_slot = slot_index[None, :] < slot_index[:, None]
    my_rank = jnp.sum(jnp.logical_and(shared_owner, earlier_slot), axis=1)
    fetched = incoming.reshape(segments * capacity, 2, head_cols)[my_owner * capacity + my_rank]
    live_slots = slot_index < counts[segment]
    frame_mask = own_ids[:, None] == window_ids[None, :]
    allowed = jnp.concatenate(
        [frame_mask, jnp.broadcast_to(live_slots[None, :], (seg_rows, slots))], axis=1
    )
    keys_all = jnp.concatenate([window_kv[:, 0], fetched[:, 0]], axis=0)
    values_all = jnp.concatenate([window_kv[:, 1], fetched[:, 1]], axis=0)
    attended = attend(proj_qkv[:, 0], keys_all, values_all, allowed)
    branch_out = jnp.dot(
        lax.all_gather(attended, "heads", axis=1, tiled=True),
        out_weight,
        preferred_element_type=jnp.float32,
    )
    own_cols = lax.dynamic_slice_in_dim(hidden, lax.axis_index("heads") * head_cols, head_cols, 1)
    mixed = (own_cols.astype(jnp.float32) + branch_out).astype(jnp.bfloat16)
    kernel_taps = depth_weight.shape[0]
    widened = extended(mixed, (("tm", 0),), kernel_taps // 2).astype(jnp.float32)
    depth_sum = jnp.zeros((seg_rows, head_cols), jnp.float32)
    for tap_index in range(kernel_taps):
        depth_sum = depth_sum + widened[tap_index : tap_index + seg_rows] * depth_weight[tap_index]
    return (mixed.astype(jnp.float32) + jax.nn.silu(depth_sum * depth_scale + depth_shift)).astype(
        jnp.bfloat16
    )


def solution(mesh):
    in_specs = (
        P(("groups", "tm"), None),
        P(None, None, "heads"),
        P("heads", None),
        P(),
        P(None, None, "heads"),
        P(None, "heads"),
        P(None, "heads"),
        P("heads"),
        P("heads"),
        P("groups"),
        P("groups", None),
        P("groups"),
        P("tm", None, "heads"),
    )
    out_specs = P(("groups", "tm"), "heads")
    return jax.shard_map(body, mesh=mesh, in_specs=in_specs, out_specs=out_specs, check_vma=False)
```

profile of v0, /device:TPU:0, one launch (start us, length us, event | category | flops | bytes accessed | tf_op | source)
XLA Modules:
  0.0 177.8 jit_solution(10112746698608492671)
XLA Ops:
  0.0 1.5 reshape.168
  1.5 3.5 %fusion.67 = f32[320,1280]{1,0:T(8,128)} fusion(bf16[128,1280]{1,0:T(8,128)(2,1)} %param.15, bf16[320,1024]{1,0:T(8,128)(2,1)S(1)} %reshape.168, bf16[1024,128]{1,0:T(8,128)(2,1)} %bitcast.72), kind=kOutput, calls=%fused_computation.123 | convolution fusion | flops 191406080 | bytes 2883584 | tf_op jit(solution)/shard_map/dot_general | solution.py:75
  4.9 36.0 %all-reduce.2 = bf16[320,1280]{1,0:T(8,128)(2,1)S(1)} all-reduce(f32[320,1280]{1,0:T(8,128)} %fusion.67), channel_id=1, replica_groups=mesh['groups'=2,'tm'=4,'heads'=4] {'heads'}, use_global_device_ids=true, to_apply=%region_0.0 | all-reduce | flops 409600 | bytes 2457600 | tf_op jit(solution)/shard_map/psum | solution.py:76
  41.0 0.2 convert_reduce_fusion
  41.2 0.4 fusion.10
  41.6 1.6 convolution_convert_fusion
  43.2 0.9 copy-done.1
  44.1 0.9 slice.292
  45.0 1.3 collective-permute-start.1
  46.2 5.4 %collective-permute-start = (bf16[320,2,320]{0,2,1:T(8,128)(2,1)}, bf16[320,2,320]{0,2,1:T(8,128)(2,1)}, u32[]{:S(2)}, u32[]{:S(2)}) collective-permute-start(bf16[320,2,320]{0,2,1:T(8,128)(2,1)} %slice.292), channel_id=1, source_target_pairs={{0,4},{4,8},{8,12},{1,5},{5,9},{9,13},{2,6},{6,10},{10,14},{3,7},{... | collective-permute-start | bytes 1228808 | tf_op jit(solution)/shard_map/ppermute | solution.py:19
  51.7 1.2 reduce-window.6
  52.9 0.2 slice_reduce_fusion
  53.1 0.2 reduce-window.9
  53.3 0.1 add_bitcast_fusion
  53.4 0.1 and_reduce_fusion
  53.5 0.1 multiply_reduce_fusion
  53.6 8.0 %scatter_custom_fusion = s32[1024]{0:T(1024)S(1)} fusion(s32[2048]{0:T(1024)S(1)} %bitcast.71, s32[2048]{0:T(1024)S(1)} %bitcast.70, s32[]{:T(128)} %constant.132.clone.1), kind=kCustom, calls=%fused_computation.193 | custom fusion | bytes 4100
  61.7 8.7 %copy.22 = bf16[2048,2,320]{2,1,0:T(2,128)(2,1)} copy(bf16[2048,2,320]{0,2,1:T(8,128)(2,1)} %param.25) | data formatting | bytes 5242880 | tf_op args[12]
  70.4 11.6 %gather_fusion = bf16[1024,2,320]{2,1,0:T(2,128)(2,1)} fusion(bf16[2048,2,320]{2,1,0:T(2,128)(2,1)} %copy.22, s32[1024]{0:T(1024)S(1)} %broadcast_clamp_fusion), kind=kCustom, calls=%fused_computation | custom fusion | bytes 2625536 | tf_op jit(solution)/shard_map/gather | solution.py:101
  81.9 4.8 %copy.23 = bf16[4,256,2,320]{1,3,2,0:T(8,128)(2,1)} copy(bf16[4,256,2,320]{3,2,1,0:T(2,128)(2,1)} %bitcast.56) | data formatting | bytes 2621440 | tf_op jit(solution)/shard_map/gather | solution.py:101
  86.7 4.6 %all-to-all-start = ((bf16[4,256,2,320]{1,3,2,0:T(8,128)(2,1)}), bf16[4,256,2,320]{1,3,2,0:T(8,128)(2,1)}, u32[]{:S(2)}, u32[]{:S(2)}) async-start(bf16[4,256,2,320]{1,3,2,0:T(8,128)(2,1)} %copy.23), calls=%async_computation | async-start | bytes 2621440 | tf_op jit(solution)/shard_map/all_to_all | solution.py:102
  91.4 0.6 dynamic_slice.20
  92.0 0.1 pad_dynamic-slice_fusion
  92.1 0.6 iota_compare_fusion.1
  92.7 0.1 dynamic_slice.18
  92.8 0.1 pad.11.clone
  92.9 0.3 convert_reduce_fusion.1
  93.2 0.7 slice_reduce_fusion.31
  93.9 0.2 broadcast_compare_fusion
  94.1 1.0 pad_add_fusion
  95.1 1.7 pad_maximum_fusion
  96.9 1.2 fusion.147
  98.1 24.9 %all-to-all-done = bf16[4,256,2,320]{1,3,2,0:T(8,128)(2,1)} async-done(((bf16[4,256,2,320]{1,3,2,0:T(8,128)(2,1)}), bf16[4,256,2,320]{1,3,2,0:T(8,128)(2,1)}, u32[]{:S(2)}, u32[]{:S(2)}) %all-to-all-start) | async-done | bytes 1310752 | tf_op jit(solution)/shard_map/all_to_all | solution.py:102
  122.9 4.9 %copy.24 = bf16[4,256,2,320]{3,2,1,0:T(2,128)(2,1)} copy(bf16[4,256,2,320]{1,3,2,0:T(8,128)(2,1)} %all-to-all-done) | data formatting | bytes 2621440 | tf_op jit(solution)/shard_map/all_to_all | solution.py:102
  127.8 4.7 %gather_fusion.1 = bf16[512,2,320]{2,1,0:T(2,128)(2,1)} fusion(bf16[1024,2,320]{2,1,0:T(2,128)(2,1)} %bitcast.57, s32[1024]{0:T(1024)S(1)} %pad_clamp_fusion), kind=kCustom, calls=%fused_computation.1 | custom fusion | bytes 1312768 | tf_op jit(solution)/shard_map/gather | solution.py:109
  132.5 3.9 %fusion.148 = (bf16[512,1,320]{2,1,0:T(2,128)(2,1)}, bf16[512,1,320]{2,1,0:T(2,128)(2,1)}) fusion(bf16[512,2,320]{2,1,0:T(2,128)(2,1)} %gather_fusion.1), kind=kLoop, calls=%fused_computation.269 | loop fusion | bytes 1310720 | tf_op jit(solution)/shard_map/slice | solution.py:116
  136.5 2.8 %copy.25 = bf16[512,1,320]{0,2,1:T(8,128)(2,1)} copy(bf16[512,1,320]{2,1,0:T(2,128)(2,1)} %get-tuple-element.42) | data formatting | bytes 655360 | tf_op jit(solution)/shard_map/slice | solution.py:116
  139.3 2.8 %copy.26 = bf16[512,1,320]{0,2,1:T(8,128)(2,1)} copy(bf16[512,1,320]{2,1,0:T(2,128)(2,1)} %get-tuple-element.43) | data formatting | bytes 655360 | tf_op jit(solution)/shard_map/slice | solution.py:115
  142.1 10.1 %fusion.150 = (f32[5,320]{1,0:T(8,128)}, f32[5,320,1472]{2,1,0:T(8,128)}) fusion(pred[320,1472]{1,0:T(8,128)(4,1)} %pad_add_fusion, bf16[320,5,64]{0,2,1:T(8,128)(2,1)S(1)} %bitcast.58, bf16[512,5,64]{0,2,1:T(8,128)(2,1)} %bitcast.62, bf16[960,5,64]{0,2,1:T(8,128)(2,1)} %bitcast.60), kind=kOutput, calls=%fused_computation.271 | convolution fusion | flops 315127232 | bytes 11045120 | tf_op jit(solution)/shard_map/sub | solution.py:44
  152.2 5.7 %fusion.14 = bf16[5,64,320]{2,1,0:T(8,128)(2,1)S(1)} fusion(f32[5,320,1472]{2,1,0:T(8,128)} %get-tuple-element.47, f32[5,320]{1,0:T(8,128)} %get-tuple-element.46, bf16[512,5,64]{0,2,1:T(8,128)(2,1)} %bitcast.61, bf16[960,5,64]{0,2,1:T(8,128)(2,1)} %bitcast.59), kind=kOutput, calls=%fused_computation.25 | convolution fusion | flops 308162560 | bytes 10574080 | tf_op jit(solution)/shard_map/hqk,khd->qhd/dot_general | solution.py:46
  157.9 9.1 %all_gather.3 = bf16[320,1280]{0,1:T(8,128)(2,1)S(1)} all-gather(bf16[320,320]{0,1:T(8,128)(2,1)S(1)} %bitcast.63), channel_id=1, replica_groups=mesh['groups'=2,'tm'=4,'heads'=4] {'heads'}, dimensions={1}, use_global_device_ids=true | all-gather | bytes 1024000 | tf_op jit(solution)/shard_map/all_gather | solution.py:119
  167.1 0.7 fusion.13
  167.9 1.3 collective-permute-start.2
  169.2 1.3 collective-permute-start.3
  170.5 1.0 slice_reduce_fusion.30
  171.5 3.2 %collective-permute-done.3 = bf16[15,320]{1,0:T(8,128)(2,1)S(1)} collective-permute-done((bf16[15,320]{1,0:T(8,128)(2,1)S(1)}, bf16[15,320]{1,0:T(8,128)(2,1)S(1)}, u32[]{:S(2)}, u32[]{:S(2)}) %collective-permute-start.3) | collective-permute-done | bytes 9632 | tf_op jit(solution)/shard_map/ppermute | solution.py:21
  174.8 0.1 maximum_convert_fusion
  175.0 2.8 %add_convert_fusion = bf16[320,320]{1,0:T(8,128)(2,1)} fusion(bf16[320,320]{1,0:T(8,128)(2,1)S(1)} %fusion.13, f32[350,320]{1,0:T(8,128)S(1)} %maximum_convert_fusion, f32[320]{0:T(512)S(1)} %copy-done.16, f32[320]{0:T(512)S(1)} %copy-done.17, f32[320]{0:T(512)S(1)} %get-tuple-element.34, f32[320]{0:T(512)S(1)} %get-tuple-element.35, ...), kind=kLoop, calls=%fused_computation.102 | loop fusion | flops 7168000 | bytes 13149440 | tf_op jit(solution)/shard_map/convert_element_type | solution.py:130
  (69 shorter events, 0.3 us)
Async XLA Ops:
  0.0 41.6 %copy-start = (bf16[1280,3,320]{0,2,1:T(8,128)(2,1)S(1)}, bf16[1280,3,320]{0,2,1:T(8,128)(2,1)}, u32[]{:S(2)}) copy-start(bf16[1280,3,320]{0,2,1:T(8,128)(2,1)} %param.17) | copy-start | bytes 7372804
  4.9 36.7 %copy-start.21 = (f32[1280]{0:T(1024)S(1)}, f32[1280]{0:T(1024)}, u32[]{:S(2)}) copy-start(f32[1280]{0:T(1024)} %param.16) | copy-start | bytes 15364
  41.6 10.0 %copy-start.3 = (s32[4,512]{1,0:T(4,128)S(1)}, s32[4,512]{1,0:T(4,128)}, u32[]{:S(2)}) copy-start(s32[4,512]{1,0:T(4,128)} %param.23) | copy-start | bytes 24580
  41.6 11.8 %copy-start.19 = (s32[2]{0:T(128)S(1)}, s32[2]{0:T(128)}, u32[]{:S(2)}) copy-start(s32[2]{0:T(128)} %constant.156) | copy-start | bytes 28
  41.6 11.9 %copy-start.18 = (s32[2]{0:T(128)S(1)}, s32[2]{0:T(128)}, u32[]{:S(2)}) copy-start(s32[2]{0:T(128)} %constant.153) | copy-start | bytes 28
  43.2 0.9 copy-start.1
  45.0 50.2 %collective-permute-start.1 = (bf16[320,2,320]{0,2,1:T(8,128)(2,1)}, bf16[320,2,320]{0,2,1:T(8,128)(2,1)}, u32[]{:S(2)}, u32[]{:S(2)}) collective-permute-start(bf16[320,2,320]{0,2,1:T(8,128)(2,1)} %slice.292), channel_id=1, source_target_pairs={{4,0},{8,4},{12,8},{5,1},{9,5},{13,9},{6,2},{10,6},{14,10},{7,3},{... | collective-permute-start | bytes 1228808 | tf_op jit(solution)/shard_map/ppermute | solution.py:21
  46.2 48.9 %collective-permute-start = (bf16[320,2,320]{0,2,1:T(8,128)(2,1)}, bf16[320,2,320]{0,2,1:T(8,128)(2,1)}, u32[]{:S(2)}, u32[]{:S(2)}) collective-permute-start(bf16[320,2,320]{0,2,1:T(8,128)(2,1)} %slice.292), channel_id=1, source_target_pairs={{0,4},{4,8},{8,12},{1,5},{5,9},{9,13},{2,6},{6,10},{10,14},{3,7},{... | collective-permute-start | bytes 1228808 | tf_op jit(solution)/shard_map/ppermute | solution.py:19
  86.7 4.7 %copy-start.22 = (s32[4]{0:T(128)S(1)}, s32[4]{0:T(128)}, u32[]{:S(2)}) copy-start(s32[4]{0:T(128)} %param.24) | copy-start | bytes 52
  86.7 5.3 %copy-start.4 = (s32[1280]{0:T(1024)S(1)}, s32[1280]{0:T(1024)}, u32[]{:S(2)}) copy-start(s32[1280]{0:T(1024)} %param.22) | copy-start | bytes 15364
  86.7 6.5 %copy-start.2 = (f32[31,320]{1,0:T(8,128)S(1)}, f32[31,320]{1,0:T(8,128)}, u32[]{:S(2)}) copy-start(f32[31,320]{1,0:T(8,128)} %param.19) | copy-start | bytes 119044
  86.7 36.2 %all-to-all-start = ((bf16[4,256,2,320]{1,3,2,0:T(8,128)(2,1)}), bf16[4,256,2,320]{1,3,2,0:T(8,128)(2,1)}, u32[]{:S(2)}, u32[]{:S(2)}) async-start(bf16[4,256,2,320]{1,3,2,0:T(8,128)(2,1)} %copy.23), calls=%async_computation | async-start | bytes 2621440 | tf_op jit(solution)/shard_map/all_to_all | solution.py:102
  132.5 9.6 %slice-start = ((bf16[320,3,320]{0,2,1:T(8,128)(2,1)}), bf16[320,1,320]{0,2,1:T(8,128)(2,1)S(1)}, s32[]{:S(2)}) async-start(bf16[320,3,320]{0,2,1:T(8,128)(2,1)} %copy-done.1), calls=%async_computation.1 | async-start | bytes 491520 | tf_op jit(solution)/shard_map/slice | solution.py:117
  152.2 14.8 %copy-start.20 = (bf16[1280,320]{0,1:T(8,128)(2,1)S(1)}, bf16[1280,320]{0,1:T(8,128)(2,1)}, u32[]{:S(2)}) copy-start(bf16[1280,320]{0,1:T(8,128)(2,1)} %param.18) | copy-start | bytes 2457604
  167.0 7.8 %copy-start.5 = (f32[320]{0:T(512)S(1)}, f32[320]{0:T(512)}, u32[]{:S(2)}) copy-start(f32[320]{0:T(512)} %get-tuple-element.13) | copy-start | bytes 3844
  167.0 7.8 %copy-start.6 = (f32[320]{0:T(512)S(1)}, f32[320]{0:T(512)}, u32[]{:S(2)}) copy-start(f32[320]{0:T(512)} %get-tuple-element.14) | copy-start | bytes 3844
  167.0 7.8 %copy-start.7 = (f32[320]{0:T(512)S(1)}, f32[320]{0:T(512)}, u32[]{:S(2)}) copy-start(f32[320]{0:T(512)} %get-tuple-element.15) | copy-start | bytes 3844
  167.0 7.8 %copy-start.8 = (f32[320]{0:T(512)S(1)}, f32[320]{0:T(512)}, u32[]{:S(2)}) copy-start(f32[320]{0:T(512)} %get-tuple-element.16) | copy-start | bytes 3844
  167.1 7.8 %copy-start.9 = (f32[320]{0:T(512)S(1)}, f32[320]{0:T(512)}, u32[]{:S(2)}) copy-start(f32[320]{0:T(512)} %get-tuple-element.17) | copy-start | bytes 3844
  167.1 7.8 %copy-start.10 = (f32[320]{0:T(512)S(1)}, f32[320]{0:T(512)}, u32[]{:S(2)}) copy-start(f32[320]{0:T(512)} %get-tuple-element.18) | copy-start | bytes 3844
  167.1 7.8 %copy-start.11 = (f32[320]{0:T(512)S(1)}, f32[320]{0:T(512)}, u32[]{:S(2)}) copy-start(f32[320]{0:T(512)} %get-tuple-element.19) | copy-start | bytes 3844
  167.1 7.8 %copy-start.12 = (f32[320]{0:T(512)S(1)}, f32[320]{0:T(512)}, u32[]{:S(2)}) copy-start(f32[320]{0:T(512)} %get-tuple-element.20) | copy-start | bytes 3844
  167.1 7.8 %copy-start.13 = (f32[320]{0:T(512)S(1)}, f32[320]{0:T(512)}, u32[]{:S(2)}) copy-start(f32[320]{0:T(512)} %get-tuple-element.21) | copy-start | bytes 3844
  167.1 7.8 %copy-start.14 = (f32[320]{0:T(512)S(1)}, f32[320]{0:T(512)}, u32[]{:S(2)}) copy-start(f32[320]{0:T(512)} %get-tuple-element.22) | copy-start | bytes 3844
  167.1 7.8 %copy-start.15 = (f32[320]{0:T(512)S(1)}, f32[320]{0:T(512)}, u32[]{:S(2)}) copy-start(f32[320]{0:T(512)} %get-tuple-element.23) | copy-start | bytes 3844
  167.1 7.8 %copy-start.16 = (f32[320]{0:T(512)S(1)}, f32[320]{0:T(512)}, u32[]{:S(2)}) copy-start(f32[320]{0:T(512)} %param.21) | copy-start | bytes 3844
  167.1 7.8 %copy-start.17 = (f32[320]{0:T(512)S(1)}, f32[320]{0:T(512)}, u32[]{:S(2)}) copy-start(f32[320]{0:T(512)} %param.20) | copy-start | bytes 3844
  167.9 3.7 %collective-permute-start.2 = (bf16[15,320]{1,0:T(8,128)(2,1)S(1)}, bf16[15,320]{1,0:T(8,128)(2,1)S(1)}, u32[]{:S(2)}, u32[]{:S(2)}) collective-permute-start(bf16[15,320]{1,0:T(8,128)(2,1)S(1)} %get-tuple-element.44), channel_id=1, source_target_pairs={{0,4},{4,8},{8,12},{1,5},{5,9},{9,13},{2,6},{6,10},{10,14},{3,7},{... | collective-permute-start | bytes 28808 | tf_op jit(solution)/shard_map/ppermute | solution.py:19
  169.2 5.6 %collective-permute-start.3 = (bf16[15,320]{1,0:T(8,128)(2,1)S(1)}, bf16[15,320]{1,0:T(8,128)(2,1)S(1)}, u32[]{:S(2)}, u32[]{:S(2)}) collective-permute-start(bf16[15,320]{1,0:T(8,128)(2,1)S(1)} %get-tuple-element.45), channel_id=1, source_target_pairs={{4,0},{8,4},{12,8},{5,1},{9,5},{13,9},{6,2},{10,6},{14,10},{7,3},{... | collective-permute-start | bytes 28808 | tf_op jit(solution)/shard_map/ppermute | solution.py:21
where the time goes:
time: 179 us; the launch traced here: 178 us
  local copies, waits for them, and re-layouts  59.6 us (33%)
  blocking collectives  45.1 us (25%)
  waiting for transfers between devices  28.1 us (16%)
  matrix products  21.5 us (12%)
  starting transfers between devices  13.8 us (8%)
  other arithmetic  9.11 us (5%)
    psum x1, blocking collectives, body(): hidden = lax.psum(partial_sum, 'heads').astype(jnp.bfloat16)  36 us
    all_to_all x1, waiting for transfers between devices, body(): lax.all_to_all(outgoing, 'tm', split_axis=0, concat_axis=0, tiled=True)  24.9 us
    unnamed x51, local copies, waits for them, and re-layouts  17.7 us
    gather x2, local copies, waits for them, and re-layouts, body(): outgoing = phrase_store[requests]  16.4 us
    sub x1, matrix products, attend(): raised = jnp.where(allowed[None], jnp.exp(scores - highest), 0.0)  10.1 us
    all_gather x1, blocking collectives, body(): lax.all_gather(attended, 'heads', axis=1, tiled=True)  9.1 us
    slice x3, local copies, waits for them, and re-layouts, body(): values_all = jnp.concatenate([window_kv[:, 1], fetched[:, 1]], axis=0)  7.92 us
    ppermute x2, starting transfers between devices, extended(): lax.ppermute(tail, axis, [(i, (i + 1) % count) for i in range(ends)])  6.66 us
  transfers between devices with their start and end apart: 5, of which 2 were waited for; matrix products, arithmetic and copies ran while one was open for 24% of the time, Pallas kernels for 0%

commit v1 on v0

v1 whole, which is shorter than its diff:
```python
import functools
import math

import jax
import jax.numpy as jnp
from jax import lax
from jax.experimental import pallas as pl
from jax.experimental.pallas import tpu as pltpu
from jax.sharding import PartitionSpec as P

HEAD_DIM = 64
EDGE = 16
BLOCKS = 2
NEG = -1e30
F32 = jnp.float32
BF16 = jnp.bfloat16


def dot_nt(a, b):
    return lax.dot_general(a, b, (((1,), (1,)), ((), ())), preferred_element_type=F32)


def dot_nn(a, b):
    return lax.dot_general(a, b, (((1,), (0,)), ((), ())), preferred_element_type=F32)


def kernel(
    segments,
    cap,
    owners_ref,
    wave_ref,
    conv_ref,
    proj_ref,
    gain_ref,
    wqkv_hbm,
    wout_hbm,
    taps_ref,
    scale_ref,
    shift_ref,
    own_ids_ref,
    win_ids_ref,
    slot_bias_ref,
    requests_ref,
    store_hbm,
    out_ref,
    store,
    wqkv,
    wout,
    picked,
    landed,
    proj_all,
    conv_all,
    conv_pre,
    hidden,
    normed,
    queries,
    kv,
    phrases,
    bias,
    attended,
    mixed,
    wide,
    load_sem,
    proj_send,
    proj_recv,
    conv_send,
    conv_recv,
    pick_send,
    pick_recv,
    kv_send,
    kv_recv,
    att_send,
    att_recv,
    mix_send,
    mix_recv,
):
    rows, cols = out_ref.shape
    slots = phrases.shape[1]
    me = lax.axis_index("heads")
    seg = lax.axis_index("tm")
    near = me + 1 - 2 * (me % 2)
    far = (me + 2) % 4

    def remote(src, dst, send, recv, **where):
        return pltpu.make_async_remote_copy(
            src_ref=src,
            dst_ref=dst,
            send_sem=send,
            recv_sem=recv,
            device_id=where,
            device_id_type=pl.DeviceIdType.MESH,
        )

    loads = [
        pltpu.make_async_copy(store_hbm, store, load_sem.at[0]),
        pltpu.make_async_copy(wqkv_hbm, wqkv, load_sem.at[1]),
        pltpu.make_async_copy(wout_hbm, wout, load_sem.at[2]),
    ]
    for load in loads:
        load.start()

    barrier = pltpu.get_barrier_semaphore()
    for peer in (near, far):
        pl.semaphore_signal(
            barrier, inc=1, device_id={"heads": peer}, device_id_type=pl.DeviceIdType.MESH
        )
    for step in range(1, segments):
        pl.semaphore_signal(
            barrier,
            inc=1,
            device_id={"tm": (seg + step) % segments},
            device_id_type=pl.DeviceIdType.MESH,
        )
    pl.semaphore_wait(barrier, segments + 1)

    proj_copies = [
        remote(proj_ref, proj_all.at[me], proj_send.at[0], proj_recv.at[0], heads=near),
        remote(proj_ref, proj_all.at[me], proj_send.at[1], proj_recv.at[1], heads=far),
        remote(proj_all.at[far], proj_all.at[far], proj_send.at[2], proj_recv.at[2], heads=near),
    ]
    proj_copies[1].start()
    proj_copies[0].start()
    proj_all[me] = proj_ref[...]

    group = conv_ref.shape[2]
    both = jnp.concatenate([conv_ref[0], conv_ref[1]], axis=1)
    taps_out = dot_nn(wave_ref[...], both)
    conv_pre[0] = taps_out[:, :group]
    conv_pre[1] = taps_out[:, group:]
    total = conv_pre[0, pl.ds(0, rows, stride=2), :] + conv_pre[1, pl.ds(1, rows, stride=2), :]
    gelu = 0.5 * total * (1.0 + lax.erf(total * math.sqrt(0.5)))
    conv_all[me] = gelu.astype(BF16)
    conv_copies = [
        remote(conv_all.at[me], conv_all.at[me], conv_send.at[0], conv_recv.at[0], heads=near),
        remote(conv_all.at[me], conv_all.at[me], conv_send.at[1], conv_recv.at[1], heads=far),
        remote(conv_all.at[far], conv_all.at[far], conv_send.at[2], conv_recv.at[2], heads=near),
    ]
    conv_copies[1].start()
    conv_copies[0].start()

    loads[0].wait()
    chunk = max(cap, 256)
    per_chunk = chunk // cap
    store_rows = store.shape[1]
    for at in range(segments * cap // chunk):
        wanted = requests_ref[0:1, at * chunk : (at + 1) * chunk]
        place = lax.broadcasted_iota(jnp.int32, (store_rows, chunk), 0)
        hot = jnp.where(place == wanted, 1.0, 0.0).astype(BF16)
        found = dot_nn(store[...], hot).astype(BF16)
        for part in range(per_chunk):
            picked[at * per_chunk + part] = found[:, part * cap : (part + 1) * cap]
    pick_copies = []
    for step in range(1, segments):
        target = (seg + step) % segments
        copy = remote(
            picked.at[target], landed.at[seg], pick_send.at[step], pick_recv.at[step], tm=target
        )
        copy.start()
        pick_copies.append(copy)
    landed[seg] = picked[seg]

    same = own_ids_ref[...] == win_ids_ref[...]
    bias[:, : 3 * rows] = jnp.where(same, 0.0, NEG)
    bias[:, 3 * rows :] = jnp.broadcast_to(slot_bias_ref[...], (rows, slots))

    conv_copies[1].wait_recv()
    conv_copies[2].start()
    proj_copies[1].wait_recv()
    proj_copies[2].start()
    conv_copies[0].wait_recv()
    proj_copies[0].wait_recv()
    conv_copies[2].wait_recv()
    proj_copies[2].wait_recv()
    conv_full = jnp.concatenate([conv_all[r] for r in range(4)], axis=1)
    weight_full = proj_all[...].reshape(4 * group, proj_ref.shape[1])
    hidden[...] = dot_nn(conv_full, weight_full).astype(BF16)

    def norm(block, carry):
        at = pl.ds(pl.multiple_of(block * 64, 64), 64)
        values = hidden[at, :].astype(F32)
        centred = values - jnp.mean(values, axis=-1, keepdims=True)
        variance = jnp.mean(centred * centred, axis=-1, keepdims=True)
        normed[at, :] = (centred * lax.rsqrt(variance + 1e-05) * gain_ref[...]).astype(BF16)
        return carry

    lax.fori_loop(0, rows // 64, norm, 0)

    loads[1].wait()
    kv[rows : 2 * rows, :cols] = dot_nt(normed[...], wqkv[1]).astype(BF16)
    kv[rows : 2 * rows, cols:] = dot_nt(normed[...], wqkv[2]).astype(BF16)
    own_kv = kv.at[pl.ds(rows, rows)]
    kv_down = remote(
        own_kv, kv.at[pl.ds(0, rows)], kv_send.at[0], kv_recv.at[0], tm=(seg + 1) % segments
    )
    kv_up = remote(
        own_kv,
        kv.at[pl.ds(2 * rows, rows)],
        kv_send.at[1],
        kv_recv.at[1],
        tm=(seg + segments - 1) % segments,
    )
    first = seg == 0
    last = seg == segments - 1
    inner_low = seg > 0
    inner_high = seg < segments - 1

    @pl.when(inner_high)
    def _():
        kv_down.start()

    @pl.when(inner_low)
    def _():
        kv_up.start()

    @pl.when(first)
    def _():
        kv[:rows, :] = jnp.zeros((rows, 2 * cols), BF16)

    @pl.when(last)
    def _():
        kv[2 * rows :, :] = jnp.zeros((rows, 2 * cols), BF16)

    queries[...] = (dot_nt(normed[...], wqkv[0]).astype(BF16) * HEAD_DIM**-0.5).astype(BF16)

    for copy in pick_copies:
        copy.wait_recv()
    for use in range(slots // cap):
        phrases[:, use * cap : (use + 1) * cap] = landed[owners_ref[use]]

    @pl.when(inner_low)
    def _():
        kv_down.wait_recv()

    @pl.when(inner_high)
    def _():
        kv_up.wait_recv()

    step_rows = rows // BLOCKS

    def att_copies(block):
        at = pl.ds(pl.multiple_of(block * step_rows, 32), step_rows)
        mine, others = attended.at[me, at], attended.at[far, at]
        return [
            remote(mine, mine, att_send.at[block, 0], att_recv.at[block, 0], heads=near),
            remote(mine, mine, att_send.at[block, 1], att_recv.at[block, 1], heads=far),
            remote(others, others, att_send.at[block, 2], att_recv.at[block, 2], heads=near),
        ]

    def forward(block):
        copies = att_copies(block)
        copies[1].wait_recv()
        copies[2].start()

    def attend(block, carry):
        at = pl.ds(pl.multiple_of(block * step_rows, 32), step_rows)
        for head in range(cols // HEAD_DIM):
            low, high = head * HEAD_DIM, (head + 1) * HEAD_DIM
            query = queries[at, low:high]
            frame_scores = dot_nt(query, kv[:, low:high]) + bias[at, : 3 * rows]
            slot_scores = dot_nn(query, phrases[low:high, :]) + bias[at, 3 * rows :]
            highest = jnp.maximum(
                jnp.max(frame_scores, axis=-1, keepdims=True),
                jnp.max(slot_scores, axis=-1, keepdims=True),
            )
            frame_raised = jnp.exp(frame_scores - highest)
            slot_raised = jnp.exp(slot_scores - highest)
            whole = jnp.sum(frame_raised, axis=-1, keepdims=True) + jnp.sum(
                slot_raised, axis=-1, keepdims=True
            )
            summed = dot_nn(frame_raised.astype(BF16), kv[:, cols + low : cols + high]) + dot_nt(
                slot_raised.astype(BF16), phrases[cols + low : cols + high, :]
            )
            attended[me, at, low:high] = (summed / whole).astype(BF16)
        copies = att_copies(block)
        copies[1].start()
        copies[0].start()

        @pl.when(block > 0)
        def _():
            forward(block - 1)

        return carry

    lax.fori_loop(0, BLOCKS, attend, 0)
    forward(BLOCKS - 1)

    loads[2].wait()
    own = hidden[:, :cols]
    for r in range(1, 4):
        own = jnp.where(me == r, hidden[:, r * cols : (r + 1) * cols], own)
    for block in range(BLOCKS):
        copies = att_copies(block)
        copies[0].wait_recv()
        copies[2].wait_recv()
    attended_full = jnp.concatenate([attended[r] for r in range(4)], axis=1)
    product = dot_nt(attended_full, wout[...])
    mixed[EDGE : EDGE + rows, :] = (own.astype(F32) + product).astype(BF16)

    mix_down = remote(
        mixed.at[pl.ds(rows, EDGE)],
        mixed.at[pl.ds(0, EDGE)],
        mix_send.at[0],
        mix_recv.at[0],
        tm=(seg + 1) % segments,
    )
    mix_up = remote(
        mixed.at[pl.ds(EDGE, EDGE)],
        mixed.at[pl.ds(EDGE + rows, EDGE)],
        mix_send.at[1],
        mix_recv.at[1],
        tm=(seg + segments - 1) % segments,
    )

    @pl.when(inner_high)
    def _():
        mix_down.start()

    @pl.when(inner_low)
    def _():
        mix_up.start()

    @pl.when(first)
    def _():
        mixed[:EDGE, :] = jnp.zeros((EDGE, cols), BF16)

    @pl.when(last)
    def _():
        mixed[EDGE + rows :, :] = jnp.zeros((EDGE, cols), BF16)

    wide[EDGE : EDGE + rows, :] = mixed[EDGE : EDGE + rows, :].astype(F32)

    for copy in proj_copies + conv_copies + pick_copies:
        copy.wait_send()
    for block in range(BLOCKS):
        for copy in att_copies(block):
            copy.wait_send()

    @pl.when(inner_high)
    def _():
        kv_down.wait_send()
        mix_down.wait_send()
        mix_up.wait_recv()

    @pl.when(inner_low)
    def _():
        kv_up.wait_send()
        mix_up.wait_send()
        mix_down.wait_recv()

    wide[:EDGE, :] = mixed[:EDGE, :].astype(F32)
    wide[EDGE + rows :, :] = mixed[EDGE + rows :, :].astype(F32)

    kernel_taps = taps_ref.shape[0]
    lead = EDGE - kernel_taps // 2
    for top in range(0, rows, 64):
        depth = jnp.zeros((64, cols), F32)
        for tap in range(kernel_taps):
            start = top + tap + lead
            depth = depth + wide[start : start + 64, :] * taps_ref[tap : tap + 1, :]
        gated = depth * scale_ref[...] + shift_ref[...]
        value = wide[EDGE + top : EDGE + top + 64, :] + gated / (1.0 + jnp.exp(-gated))
        out_ref[top : top + 64, :] = value.astype(BF16)


def body(
    wave_feats,
    conv_weight,
    proj_weight,
    ln_gain,
    qkv_weight,
    out_weight,
    depth_weight,
    depth_scale,
    depth_shift,
    seg_ids,
    phrase_ids,
    counts,
    phrase_store,
):
    rows = wave_feats.shape[0] // 2
    cols = qkv_weight.shape[2]
    width = qkv_weight.shape[0]
    group = proj_weight.shape[0]
    segment = lax.axis_index("tm")
    segments = lax.axis_size("tm")
    slots = phrase_ids.shape[1]
    cap = 2 * slots // segments
    store_rows = phrase_store.shape[0]

    padded_ids = jnp.pad(seg_ids, (rows, rows), constant_values=-1)
    win_ids = lax.dynamic_slice_in_dim(padded_ids, segment * rows, 3 * rows, 0)
    own_ids = lax.dynamic_slice_in_dim(seg_ids, segment * rows, rows, 0)

    owners = lax.div(phrase_ids, store_rows)
    local = phrase_ids - owners * store_rows
    order = jnp.arange(slots, dtype=jnp.int32)
    earlier = order[:, None] < order[None, :]
    held = owners == segment
    rank = jnp.sum(
        jnp.logical_and(held[:, :, None], earlier[None]).astype(jnp.int32), axis=1
    )
    rank = jnp.where(held, rank, cap)
    ranks = jnp.arange(cap, dtype=jnp.int32)
    requests = jnp.sum(
        jnp.where(rank[:, :, None] == ranks[None, None, :], local[:, :, None], 0), axis=1
    ).reshape(1, segments * cap)

    my_owner = lax.dynamic_index_in_dim(owners, segment, 0, keepdims=False)
    every = jnp.arange(segments, dtype=jnp.int32)
    listed = my_owner[None, :] == every[:, None]
    live = jnp.sum(
        jnp.logical_and(listed, order[None, :] < counts[segment]).astype(jnp.int32), axis=1
    )
    present = jnp.any(listed, axis=1)
    before = jnp.sum(
        jnp.logical_and(present[None, :], every[None, :] < every[:, None]).astype(jnp.int32), axis=1
    )
    uses = jnp.arange(slots // cap, dtype=jnp.int32)
    chosen = jnp.logical_and(present[None, :], before[None, :] == uses[:, None]).astype(jnp.int32)
    owner_list = jnp.sum(chosen * every[None, :], axis=1)
    live_list = jnp.sum(chosen * live[None, :], axis=1)
    slot_bias = jnp.where(ranks[None, :] < live_list[:, None], 0.0, NEG).reshape(1, slots)

    vmem = pl.BlockSpec(memory_space=pltpu.VMEM)
    hbm = pl.BlockSpec(memory_space=pl.ANY)
    smem = pl.BlockSpec(memory_space=pltpu.SMEM)
    dma = pltpu.SemaphoreType.DMA
    return pl.pallas_call(
        functools.partial(kernel, segments, cap),
        out_shape=jax.ShapeDtypeStruct((rows, cols), BF16),
        in_specs=[smem] + [vmem] * 4 + [hbm] * 2 + [vmem] * 7 + [hbm],
        out_specs=vmem,
        scratch_shapes=[
            pltpu.VMEM((2 * cols, store_rows), BF16),
            pltpu.VMEM((3, cols, width), BF16),
            pltpu.VMEM((cols, width), BF16),
            pltpu.VMEM((segments, 2 * cols, cap), BF16),
            pltpu.VMEM((segments, 2 * cols, cap), BF16),
            pltpu.VMEM((4, group, width), BF16),
            pltpu.VMEM((4, rows, group), BF16),
            pltpu.VMEM((2, 2 * rows, group), F32),
            pltpu.VMEM((rows, width), BF16),
            pltpu.VMEM((rows, width), BF16),
            pltpu.VMEM((rows, cols), BF16),
            pltpu.VMEM((3 * rows, 2 * cols), BF16),
            pltpu.VMEM((2 * cols, slots), BF16),
            pltpu.VMEM((rows, 3 * rows + slots), F32),
            pltpu.VMEM((4, rows, cols), BF16),
            pltpu.VMEM((rows + 2 * EDGE, cols), BF16),
            pltpu.VMEM((rows + 2 * EDGE, cols), F32),
            dma((3,)),
            dma((3,)),
            dma((3,)),
            dma((3,)),
            dma((3,)),
            dma((segments,)),
            dma((segments,)),
            dma((2,)),
            dma((2,)),
            dma((BLOCKS, 3)),
            dma((BLOCKS, 3)),
            dma((2,)),
            dma((2,)),
        ],
        compiler_params=pltpu.CompilerParams(
            collective_id=0, has_side_effects=True, vmem_limit_bytes=56 * 2**20
        ),
        name="segment_block",
    )(
        owner_list,
        wave_feats,
        conv_weight,
        proj_weight,
        ln_gain.reshape(1, width),
        jnp.transpose(qkv_weight, (1, 2, 0)),
        jnp.transpose(out_weight, (1, 0)),
        depth_weight,
        depth_scale.reshape(1, cols),
        depth_shift.reshape(1, cols),
        own_ids.reshape(rows, 1),
        win_ids.reshape(1, 3 * rows),
        slot_bias,
        requests,
        jnp.transpose(phrase_store, (1, 2, 0)).reshape(2 * cols, store_rows),
    )


def solution(mesh):
    in_specs = (
        P(("groups", "tm"), None),
        P(None, None, "heads"),
        P("heads", None),
        P(),
        P(None, None, "heads"),
        P(None, "heads"),
        P(None, "heads"),
        P("heads"),
        P("heads"),
        P("groups"),
        P("groups", None),
        P("groups"),
        P("tm", None, "heads"),
    )
    out_specs = P(("groups", "tm"), "heads")
    return jax.shard_map(body, mesh=mesh, in_specs=in_specs, out_specs=out_specs, check_vma=False)
```

time: 179 us -> 80.3 us (0.45)
  Pallas kernels: 0 us -> 64.4 us
  local copies, waits for them, and re-layouts: 59.6 us -> 10.9 us
  blocking collectives: 45.1 us -> 0 us
  waiting for transfers between devices: 28.1 us -> 0 us
  matrix products: 21.5 us -> 0 us
  starting transfers between devices: 13.8 us -> 0 us
  other arithmetic: 9.11 us -> 4.42 us
    pallas_call x0 -> x1, Pallas kernels: none -> 64.4 us  [body(): pl.pallas_call(functools.partial(kernel, segments, cap), out_shape=jax.Sh...]
    psum x1 -> x0, blocking collectives: 36 us -> none  [body(): hidden = lax.psum(partial_sum, 'heads').astype(jnp.bfloat16)]
    all_to_all x1 -> x0, waiting for transfers between devices: 24.9 us -> none  [body(): lax.all_to_all(outgoing, 'tm', split_axis=0, concat_axis=0, tiled=True)]
    gather x3 -> x0, local copies, waits for them, and re-layouts: 21.1 us -> none  [the longest x2 16.4 us: body(): outgoing = phrase_store[requests]]
    unnamed x51 -> x3, local copies, waits for them, and re-layouts: 17.7 us -> 2.86 us
    slice x11 -> x0, local copies, waits for them, and re-layouts: 13.6 us -> none  [the longest x3 7.92 us: body(): values_all = jnp.concatenate([window_kv[:, 1], fetched[:, 1]], axis=0)]
    dot_general x4 -> x0, matrix products: 11.4 us -> none  [the longest x1 5.7 us: attend(): jnp.einsum('hqk,khd->qhd', weights, value_heads, preferred_element_type=j...]
    sub x1 -> x0, matrix products: 10.1 us -> none  [attend(): raised = jnp.where(allowed[None], jnp.exp(scores - highest), 0.0)]
  transfers between devices with their start and end apart: 5 -> 0, of which waited for: 2 -> 0; matrix products, arithmetic and copies ran while one was open for 24% -> 0% of each run, Pallas kernels for 0% -> 0%
where the time goes in v1:
time: 80.3 us; the launch traced here: 79.8 us
  Pallas kernels  64.4 us (80%)
  local copies, waits for them, and re-layouts  10.9 us (14%)
  other arithmetic  4.42 us (6%)
    pallas_call x1, Pallas kernels, body(): pl.pallas_call(functools.partial(kernel, segments, cap), out_shape=jax.Sh...  64.4 us
    unnamed x3, local copies, waits for them, and re-layouts  2.86 us

profile of v1, /device:TPU:0, one launch (start us, length us, event | category | flops | bytes accessed | tf_op | source)
XLA Modules:
  0.0 79.8 jit_solution(12761091054411818019)
XLA Ops:
  0.0 1.2 %dynamic_slice.16 = s32[1]{0:T(128)} dynamic-slice(s32[4]{0:T(128)} %param.24, s32[]{:T(128)S(6)} %select_n.33), dynamic_slice_sizes={1} | dynamic-slice | bytes 12 | tf_op jit(solution)/shard_map/dynamic_slice | solution.py:412
  1.2 0.6 iota_compare_fusion.3
  1.9 1.3 %reshape.75.scale_ref = f32[1,320]{1,0:T(1,128)} reshape(f32[320]{0:T(512)} %param.20) | data formatting | bytes 2560 | tf_op jit(solution)/shard_map/reshape | solution.py:478
  3.2 1.3 %reshape.76.shift_ref = f32[1,320]{1,0:T(1,128)} reshape(f32[320]{0:T(512)} %param.21) | data formatting | bytes 2560 | tf_op jit(solution)/shard_map/reshape | solution.py:479
  4.4 0.8 dynamic_slice.14
  5.2 0.7 broadcast_compare_fusion
  5.9 1.4 %pad_dynamic-slice_fusion = s32[960]{0:T(1024)} fusion(s32[]{:T(128)S(6)} %select_n.35, s32[1280]{0:T(1024)} %param.22), kind=kLoop, calls=%fused_computation.9 | loop fusion | bytes 8964 | tf_op jit(solution)/shard_map/dynamic_slice | solution.py:391
  7.3 1.3 %reshape.74.gain_ref = f32[1,1280]{1,0:T(1,128)} reshape(f32[1280]{0:T(1024)} %param.16) | data formatting | bytes 10240 | tf_op jit(solution)/shard_map/reshape | solution.py:474
  8.6 0.8 reshape.81.own_ids_ref
  9.4 0.1 iota_compare_fusion.1
  9.4 0.5 convert_reduce_fusion
  9.9 0.7 multiply_subtract_fusion
  10.7 0.7 select_reduce_fusion
  11.4 0.6 copy.17
  12.0 0.1 convert_reduce_fusion.1
  12.1 0.1 fusion.2
  12.2 0.1 convert_reduce_fusion.2
  12.3 0.6 select_reduce_fusion.1
  13.0 0.1 fusion.3
  13.1 0.6 copy.16
  13.7 64.4 %segment_block.1 = bf16[320,320]{1,0:T(8,128)(2,1)} custom-call(s32[2]{0:T(128)} %get-tuple-element.6.owners_ref, bf16[640,512]{1,0:T(8,128)(2,1)} %wave_ref.1, bf16[2,512,128]{2,1,0:T(8,128)(2,1)} %conv_ref.1, bf16[128,1280]{1,0:T(8,128)(2,1)} %proj_ref.1, f32[1,1280]{1,0:T(1,128)} %reshape.74.gain_ref, bf16[3,320,1280]{2,1,0:T(8,128)(2,1)} %bitcast.16, ...), custom_call_target="tpu_custom_call" | custom-call | tf_op jit(solution)/shard_map/segment_block/pallas_call | solution.py:428
  78.1 1.7 %copy.19 = bf16[320,320]{1,0:T(8,128)(2,1)} copy(bf16[320,320]{1,0:T(8,128)(2,1)} %segment_block.1) | data formatting | bytes 409600
  (1 shorter events, 0.0 us)

commit v2 on v1

--- a/solution.py
+++ b/solution.py
@@ -27,7 +27,7 @@
 def kernel(
     segments,
     cap,
-    owners_ref,
+    counts_ref,
     wave_ref,
     conv_ref,
     proj_ref,
@@ -37,10 +37,8 @@
     taps_ref,
     scale_ref,
     shift_ref,
-    own_ids_ref,
-    win_ids_ref,
-    slot_bias_ref,
-    requests_ref,
+    frame_ids_ref,
+    phrase_ids_ref,
     store_hbm,
     out_ref,
     store,
@@ -58,8 +56,15 @@
     phrases,
     bias,
     attended,
+    partial,
+    stats,
     mixed,
     wide,
+    window,
+    slot_bias,
+    ranks,
+    low_part,
+    high_part,
     load_sem,
     proj_send,
     proj_recv,
@@ -122,6 +127,54 @@
     proj_copies[0].start()
     proj_all[me] = proj_ref[...]
 
+    store_rows = store.shape[1]
+    ids = phrase_ids_ref[...]
+    offset = ids - seg * store_rows
+    held = jnp.logical_and(offset >= 0, offset < store_rows)
+    list_shape = (slots, slots)
+    earlier = lax.broadcasted_iota(jnp.int32, list_shape, 0) < lax.broadcasted_iota(
+        jnp.int32, list_shape, 1
+    )
+    rank = dot_nn(jnp.where(held, 1.0, 0.0).astype(BF16), jnp.where(earlier, 1.0, 0.0).astype(BF16))
+    ranks[...] = jnp.where(held, rank, -1.0)
+    offset = jnp.where(held, offset, 0)
+    low_part[...] = (offset & 255).astype(F32)
+    high_part[...] = lax.shift_right_logical(offset, 8).astype(F32)
+
+    def pick_step(turn):
+        return lax.rem(segments // 2 + turn, segments)
+
+    def pick(turn, carry):
+        target = lax.rem(seg + pick_step(turn), segments)
+        line = pl.ds(target, 1)
+        slot = lax.broadcasted_iota(jnp.int32, (cap, slots), 0).astype(F32)
+        match = jnp.where(slot == ranks[line, :], 1.0, 0.0).astype(BF16)
+        lower = jnp.broadcast_to(low_part[line, :], (8, slots)).astype(BF16)
+        upper = jnp.broadcast_to(high_part[line, :], (8, slots)).astype(BF16)
+        wanted = dot_nt(lower, match) + 256.0 * dot_nt(upper, match)
+        place = lax.broadcasted_iota(jnp.int32, (store_rows, cap), 0)
+        hot = jnp.where(place == wanted[0:1, :].astype(jnp.int32), 1.0, 0.0).astype(BF16)
+        picked[target] = dot_nn(store[...], hot).astype(BF16)
+        return carry
+
+    def pick_copy(turn):
+        step = pick_step(turn)
+        target = lax.rem(seg + step, segments)
+        return remote(
+            picked.at[target], landed.at[seg], pick_send.at[step], pick_recv.at[step], tm=target
+        )
+
+    own_turn = segments - segments // 2
+    early = max(1, segments // 4)
+    loads[0].wait()
+    lax.fori_loop(0, early, pick, 0)
+
+    def send_pick(turn, carry):
+        pick_copy(turn).start()
+        return carry
+
+    lax.fori_loop(0, early, send_pick, 0)
+
     group = conv_ref.shape[2]
     both = jnp.concatenate([conv_ref[0], conv_ref[1]], axis=1)
     taps_out = dot_nn(wave_ref[...], both)
@@ -138,30 +191,39 @@
     conv_copies[1].start()
     conv_copies[0].start()
 
-    loads[0].wait()
-    chunk = max(cap, 256)
-    per_chunk = chunk // cap
-    store_rows = store.shape[1]
-    for at in range(segments * cap // chunk):
-        wanted = requests_ref[0:1, at * chunk : (at + 1) * chunk]
-        place = lax.broadcasted_iota(jnp.int32, (store_rows, chunk), 0)
-        hot = jnp.where(place == wanted, 1.0, 0.0).astype(BF16)
-        found = dot_nn(store[...], hot).astype(BF16)
-        for part in range(per_chunk):
-            picked[at * per_chunk + part] = found[:, part * cap : (part + 1) * cap]
-    pick_copies = []
-    for step in range(1, segments):
-        target = (seg + step) % segments
-        copy = remote(
-            picked.at[target], landed.at[seg], pick_send.at[step], pick_recv.at[step], tm=target
+    lax.fori_loop(early, segments, pick, 0)
+    landed[seg] = picked[seg]
+
+    own_line = frame_ids_ref[pl.ds(seg, 1), :]
+    prev_line = frame_ids_ref[pl.ds(jnp.maximum(seg - 1, 0), 1), :]
+    next_line = frame_ids_ref[pl.ds(jnp.minimum(seg + 1, segments - 1), 1), :]
+    window[:, :rows] = jnp.where(seg > 0, prev_line, -1)
+    window[:, rows : 2 * rows] = own_line
+    window[:, 2 * rows :] = jnp.where(seg < segments - 1, next_line, -1)
+    square = (rows, rows)
+    diagonal = lax.broadcasted_iota(jnp.int32, square, 0) == lax.broadcasted_iota(
+        jnp.int32, square, 1
+    )
+    own_column = jnp.sum(
+        jnp.where(diagonal, own_line.astype(F32), 0.0), axis=1, keepdims=True
+    ).astype(jnp.int32)
+    bias[...] = jnp.where(own_column == window[...], 0.0, NEG)
+
+    my_ids = phrase_ids_ref[pl.ds(seg, 1), :]
+    live = lax.broadcasted_iota(jnp.int32, (1, slots), 1) < counts_ref[seg]
+    owners = []
+    least = 0
+    for use in range(slots // cap):
+        smallest = jnp.min(jnp.where(my_ids >= least, my_ids, segments * store_rows - 1))
+        owner = smallest // store_rows
+        owners.append(owner)
+        least = (owner + 1) * store_rows
+        listed = jnp.logical_and(my_ids >= owner * store_rows, my_ids < least)
+        number = jnp.sum(
+            jnp.where(jnp.logical_and(listed, live), 1.0, 0.0), axis=1, keepdims=True
         )
-        copy.start()
-        pick_copies.append(copy)
-    landed[seg] = picked[seg]
-
-    same = own_ids_ref[...] == win_ids_ref[...]
-    bias[:, : 3 * rows] = jnp.where(same, 0.0, NEG)
-    bias[:, 3 * rows :] = jnp.broadcast_to(slot_bias_ref[...], (rows, slots))
+        place = lax.broadcasted_iota(jnp.int32, (1, cap), 1).astype(F32)
+        slot_bias[:, use * cap : (use + 1) * cap] = jnp.where(place < number, 0.0, NEG)
 
     conv_copies[1].wait_recv()
     conv_copies[2].start()
@@ -180,7 +242,7 @@
         values = hidden[at, :].astype(F32)
         centred = values - jnp.mean(values, axis=-1, keepdims=True)
         variance = jnp.mean(centred * centred, axis=-1, keepdims=True)
-        normed[at, :] = (centred * lax.rsqrt(variance + 1e-05) * gain_ref[...]).astype(BF16)
+        normed[at, :] = (centred * lax.rsqrt(variance + 1e-05) * gain_ref[...][None, :]).astype(BF16)
         return carry
 
     lax.fori_loop(0, rows // 64, norm, 0)
@@ -220,13 +282,17 @@
     def _():
         kv[2 * rows :, :] = jnp.zeros((rows, 2 * cols), BF16)
 
+    def send_late(turn, carry):
+        @pl.when(turn != own_turn)
+        def _():
+            pick_copy(turn).start()
+
+        return carry
+
+    lax.fori_loop(early, segments, send_late, 0)
+
     queries[...] = (dot_nt(normed[...], wqkv[0]).astype(BF16) * HEAD_DIM**-0.5).astype(BF16)
 
-    for copy in pick_copies:
-        copy.wait_recv()
-    for use in range(slots // cap):
-        phrases[:, use * cap : (use + 1) * cap] = landed[owners_ref[use]]
-
     @pl.when(inner_low)
     def _():
         kv_down.wait_recv()
@@ -235,7 +301,30 @@
     def _():
         kv_up.wait_recv()
 
+    heads = cols // HEAD_DIM
     step_rows = rows // BLOCKS
+
+    def attend_frames(block, carry):
+        at = pl.ds(pl.multiple_of(block * step_rows, 32), step_rows)
+        for head in range(heads):
+            low, high = head * HEAD_DIM, (head + 1) * HEAD_DIM
+            scores = dot_nt(queries[at, low:high], kv[:, low:high]) + bias[at, :]
+            highest = jnp.max(scores, axis=-1, keepdims=True)
+            raised = jnp.exp(scores - highest)
+            stats[head, 0, at, :] = highest
+            stats[head, 1, at, :] = jnp.sum(raised, axis=-1, keepdims=True)
+            partial[head, at, :] = dot_nn(raised.astype(BF16), kv[:, cols + low : cols + high])
+        return carry
+
+    lax.fori_loop(0, BLOCKS, attend_frames, 0)
+
+    def wait_pick(step, carry):
+        pick_copy(lax.rem(step + own_turn, segments)).wait_recv()
+        return carry
+
+    lax.fori_loop(1, segments, wait_pick, 0)
+    for use, owner in enumerate(owners):
+        phrases[:, use * cap : (use + 1) * cap] = landed[owner]
 
     def att_copies(block):
         at = pl.ds(pl.multiple_of(block * step_rows, 32), step_rows)
@@ -253,22 +342,16 @@
 
     def attend(block, carry):
         at = pl.ds(pl.multiple_of(block * step_rows, 32), step_rows)
-        for head in range(cols // HEAD_DIM):
+        for head in range(heads):
             low, high = head * HEAD_DIM, (head + 1) * HEAD_DIM
-            query = queries[at, low:high]
-            frame_scores = dot_nt(query, kv[:, low:high]) + bias[at, : 3 * rows]
-            slot_scores = dot_nn(query, phrases[low:high, :]) + bias[at, 3 * rows :]
-            highest = jnp.maximum(
-                jnp.max(frame_scores, axis=-1, keepdims=True),
-                jnp.max(slot_scores, axis=-1, keepdims=True),
-            )
-            frame_raised = jnp.exp(frame_scores - highest)
-            slot_raised = jnp.exp(slot_scores - highest)
-            whole = jnp.sum(frame_raised, axis=-1, keepdims=True) + jnp.sum(
-                slot_raised, axis=-1, keepdims=True
-            )
-            summed = dot_nn(frame_raised.astype(BF16), kv[:, cols + low : cols + high]) + dot_nt(
-                slot_raised.astype(BF16), phrases[cols + low : cols + high, :]
+            scores = dot_nn(queries[at, low:high], phrases[low:high, :]) + slot_bias[...]
+            before = stats[head, 0, at, :]
+            highest = jnp.maximum(before, jnp.max(scores, axis=-1, keepdims=True))
+            raised = jnp.exp(scores - highest)
+            shrink = jnp.exp(before - highest)
+            whole = stats[head, 1, at, :] * shrink + jnp.sum(raised, axis=-1, keepdims=True)
+            summed = partial[head, at, :] * shrink + dot_nt(
+                raised.astype(BF16), phrases[cols + low : cols + high, :]
             )
             attended[me, at, low:high] = (summed / whole).astype(BF16)
         copies = att_copies(block)
@@ -329,8 +412,14 @@
 
     wide[EDGE : EDGE + rows, :] = mixed[EDGE : EDGE + rows, :].astype(F32)
 
-    for copy in proj_copies + conv_copies + pick_copies:
+    for copy in proj_copies + conv_copies:
         copy.wait_send()
+
+    def wait_sent(step, carry):
+        pick_copy(lax.rem(step + own_turn, segments)).wait_send()
+        return carry
+
+    lax.fori_loop(1, segments, wait_sent, 0)
     for block in range(BLOCKS):
         for copy in att_copies(block):
             copy.wait_send()
@@ -357,7 +446,7 @@
         for tap in range(kernel_taps):
             start = top + tap + lead
             depth = depth + wide[start : start + 64, :] * taps_ref[tap : tap + 1, :]
-        gated = depth * scale_ref[...] + shift_ref[...]
+        gated = depth * scale_ref[...][None, :] + shift_ref[...][None, :]
         value = wide[EDGE + top : EDGE + top + 64, :] + gated / (1.0 + jnp.exp(-gated))
         out_ref[top : top + 64, :] = value.astype(BF16)
 
@@ -381,45 +470,10 @@
     cols = qkv_weight.shape[2]
     width = qkv_weight.shape[0]
     group = proj_weight.shape[0]
-    segment = lax.axis_index("tm")
     segments = lax.axis_size("tm")
     slots = phrase_ids.shape[1]
     cap = 2 * slots // segments
     store_rows = phrase_store.shape[0]
-
-    padded_ids = jnp.pad(seg_ids, (rows, rows), constant_values=-1)
-    win_ids = lax.dynamic_slice_in_dim(padded_ids, segment * rows, 3 * rows, 0)
-    own_ids = lax.dynamic_slice_in_dim(seg_ids, segment * rows, rows, 0)
-
-    owners = lax.div(phrase_ids, store_rows)
-    local = phrase_ids - owners * store_rows
-    order = jnp.arange(slots, dtype=jnp.int32)
-    earlier = order[:, None] < order[None, :]
-    held = owners == segment
-    rank = jnp.sum(
-        jnp.logical_and(held[:, :, None], earlier[None]).astype(jnp.int32), axis=1
-    )
-    rank = jnp.where(held, rank, cap)
-    ranks = jnp.arange(cap, dtype=jnp.int32)
-    requests = jnp.sum(
-        jnp.where(rank[:, :, None] == ranks[None, None, :], local[:, :, None], 0), axis=1
-    ).reshape(1, segments * cap)
-
-    my_owner = lax.dynamic_index_in_dim(owners, segment, 0, keepdims=False)
-    every = jnp.arange(segments, dtype=jnp.int32)
-    listed = my_owner[None, :] == every[:, None]
-    live = jnp.sum(
-        jnp.logical_and(listed, order[None, :] < counts[segment]).astype(jnp.int32), axis=1
-    )
-    present = jnp.any(listed, axis=1)
-    before = jnp.sum(
-        jnp.logical_and(present[None, :], every[None, :] < every[:, None]).astype(jnp.int32), axis=1
-    )
-    uses = jnp.arange(slots // cap, dtype=jnp.int32)
-    chosen = jnp.logical_and(present[None, :], before[None, :] == uses[:, None]).astype(jnp.int32)
-    owner_list = jnp.sum(chosen * every[None, :], axis=1)
-    live_list = jnp.sum(chosen * live[None, :], axis=1)
-    slot_bias = jnp.where(ranks[None, :] < live_list[:, None], 0.0, NEG).reshape(1, slots)
 
     vmem = pl.BlockSpec(memory_space=pltpu.VMEM)
     hbm = pl.BlockSpec(memory_space=pl.ANY)
@@ -428,7 +482,7 @@
     return pl.pallas_call(
         functools.partial(kernel, segments, cap),
         out_shape=jax.ShapeDtypeStruct((rows, cols), BF16),
-        in_specs=[smem] + [vmem] * 4 + [hbm] * 2 + [vmem] * 7 + [hbm],
+        in_specs=[smem] + [vmem] * 4 + [hbm] * 2 + [vmem] * 5 + [hbm],
         out_specs=vmem,
         scratch_shapes=[
             pltpu.VMEM((2 * cols, store_rows), BF16),
@@ -444,10 +498,17 @@
             pltpu.VMEM((rows, cols), BF16),
             pltpu.VMEM((3 * rows, 2 * cols), BF16),
             pltpu.VMEM((2 * cols, slots), BF16),
-            pltpu.VMEM((rows, 3 * rows + slots), F32),
+            pltpu.VMEM((rows, 3 * rows), F32),
             pltpu.VMEM((4, rows, cols), BF16),
+            pltpu.VMEM((cols // HEAD_DIM, rows, HEAD_DIM), F32),
+            pltpu.VMEM((cols // HEAD_DIM, 2, rows, 1), F32),
             pltpu.VMEM((rows + 2 * EDGE, cols), BF16),
             pltpu.VMEM((rows + 2 * EDGE, cols), F32),
+            pltpu.VMEM((1, 3 * rows), jnp.int32),
+            pltpu.VMEM((1, slots), F32),
+            pltpu.VMEM((segments, slots), F32),
+            pltpu.VMEM((segments, slots), F32),
+            pltpu.VMEM((segments, slots), F32),
             dma((3,)),
             dma((3,)),
             dma((3,)),
@@ -467,20 +528,18 @@
         ),
         name="segment_block",
     )(
-        owner_list,
+        counts,
         wave_feats,
         conv_weight,
         proj_weight,
-        ln_gain.reshape(1, width),
+        ln_gain,
         jnp.transpose(qkv_weight, (1, 2, 0)),
         jnp.transpose(out_weight, (1, 0)),
         depth_weight,
-        depth_scale.reshape(1, cols),
-        depth_shift.reshape(1, cols),
-        own_ids.reshape(rows, 1),
-        win_ids.reshape(1, 3 * rows),
-        slot_bias,
-        requests,
+        depth_scale,
+        depth_shift,
+        seg_ids.reshape(segments, rows),
+        phrase_ids,
         jnp.transpose(phrase_store, (1, 2, 0)).reshape(2 * cols, store_rows),
     )
 

time: 80.3 us -> 64.9 us (0.81)
  local copies, waits for them, and re-layouts: 10.9 us -> 3.03 us
  other arithmetic: 4.42 us -> 0 us
  Pallas kernels: 64.4 us -> 61.6 us
    dynamic_slice x4 -> x0, local copies, waits for them, and re-layouts: 3.39 us -> none  [the longest x1 1.37 us: body(): win_ids = lax.dynamic_slice_in_dim(padded_ids, segment * rows, 3 * rows, 0)]
    reshape x4 -> x1, local copies, waits for them, and re-layouts: 4.61 us -> 1.36 us  [body(): seg_ids.reshape(segments, rows)]
    pallas_call x1, Pallas kernels: 64.4 us -> 61.6 us  [body(): pl.pallas_call(functools.partial(kernel, segments, cap), out_shape=jax.Sh...]
    reduce_sum x5 -> x0, other arithmetic: 2.08 us -> none  [the longest x1 0.71 us: body(): jnp.sum(jnp.where(rank[:, :, None] == ranks[None, None, :], local[:, :, N...]
    unnamed x3 -> x1, local copies, waits for them, and re-layouts: 2.86 us -> 1.66 us
where the time goes in v2:
time: 64.9 us; the launch traced here: 64.7 us
  Pallas kernels  61.6 us (95%)
  local copies, waits for them, and re-layouts  3.03 us (5%)
    pallas_call x1, Pallas kernels, body(): pl.pallas_call(functools.partial(kernel, segments, cap), out_shape=jax.Sh...  61.6 us
    unnamed x1, local copies, waits for them, and re-layouts  1.66 us
    reshape x1, local copies, waits for them, and re-layouts, body(): seg_ids.reshape(segments, rows)  1.36 us

profile of v2, /device:TPU:0, one launch (start us, length us, event | category | flops | bytes accessed | tf_op | source)
XLA Modules:
  0.0 64.7 jit_solution(2894277260742322991)
XLA Ops:
  0.0 1.4 %reshape.6.frame_ids_ref = s32[4,320]{1,0:T(4,128)} reshape(s32[1280]{0:T(1024)} %param.22) | data formatting | bytes 10240 | tf_op jit(solution)/shard_map/reshape | solution.py:541
  1.4 61.6 %segment_block.1 = bf16[320,320]{1,0:T(8,128)(2,1)} custom-call(s32[4]{0:T(128)} %counts_ref.1, bf16[640,512]{1,0:T(8,128)(2,1)} %wave_ref.1, bf16[2,512,128]{2,1,0:T(8,128)(2,1)} %conv_ref.1, bf16[128,1280]{1,0:T(8,128)(2,1)} %proj_ref.1, f32[1280]{0:T(1024)} %gain_ref.1, bf16[3,320,1280]{2,1,0:T(8,128)(2,1)} %bitcast.6, bf16[320,1280]{1,0:T(8,128)(2,1)} %bitcast.7, ...), custom_call_target="tpu_custom_call" | custom-call | tf_op jit(solution)/shard_map/segment_block/pallas_call | solution.py:482
  63.0 1.7 %copy.15 = bf16[320,320]{1,0:T(8,128)(2,1)} copy(bf16[320,320]{1,0:T(8,128)(2,1)} %segment_block.1) | data formatting | bytes 409600

commit v3 on v2

--- a/solution.py
+++ b/solution.py
@@ -191,7 +191,17 @@
     conv_copies[1].start()
     conv_copies[0].start()
 
-    lax.fori_loop(early, segments, pick, 0)
+    def pick_send_on(turn, carry):
+        pick(turn, carry)
+
+        @pl.when(turn != own_turn)
+        def _():
+            pick_copy(turn).start()
+
+        return carry
+
+    lax.fori_loop(early, segments // 2, pick_send_on, 0)
+    lax.fori_loop(segments // 2, segments, pick, 0)
     landed[seg] = picked[seg]
 
     own_line = frame_ids_ref[pl.ds(seg, 1), :]
@@ -289,7 +299,7 @@
 
         return carry
 
-    lax.fori_loop(early, segments, send_late, 0)
+    lax.fori_loop(segments // 2, segments, send_late, 0)
 
     queries[...] = (dot_nt(normed[...], wqkv[0]).astype(BF16) * HEAD_DIM**-0.5).astype(BF16)
 

time: 64.9 us -> 69.8 us (1.076)
  Pallas kernels: 61.6 us -> 66.5 us
    pallas_call x1, Pallas kernels: 61.6 us -> 66.5 us  [body(): pl.pallas_call(functools.partial(kernel, segments, cap), out_shape=jax.Sh...]
where the time goes in v3:
time: 69.8 us; the launch traced here: 69.6 us
  Pallas kernels  66.5 us (95%)
  local copies, waits for them, and re-layouts  3.03 us (4%)
    pallas_call x1, Pallas kernels, body(): pl.pallas_call(functools.partial(kernel, segments, cap), out_shape=jax.Sh...  66.5 us
    unnamed x1, local copies, waits for them, and re-layouts  1.66 us

profile of v3, /device:TPU:0, one launch (start us, length us, event | category | flops | bytes accessed | tf_op | source)
XLA Modules:
  0.0 69.6 jit_solution(6875326414842981228)
XLA Ops:
  0.0 1.4 %reshape.6.frame_ids_ref = s32[4,320]{1,0:T(4,128)} reshape(s32[1280]{0:T(1024)} %param.22) | data formatting | bytes 10240 | tf_op jit(solution)/shard_map/reshape | solution.py:551
  1.4 66.5 %segment_block.1 = bf16[320,320]{1,0:T(8,128)(2,1)} custom-call(s32[4]{0:T(128)} %counts_ref.1, bf16[640,512]{1,0:T(8,128)(2,1)} %wave_ref.1, bf16[2,512,128]{2,1,0:T(8,128)(2,1)} %conv_ref.1, bf16[128,1280]{1,0:T(8,128)(2,1)} %proj_ref.1, f32[1280]{0:T(1024)} %gain_ref.1, bf16[3,320,1280]{2,1,0:T(8,128)(2,1)} %bitcast.6, bf16[320,1280]{1,0:T(8,128)(2,1)} %bitcast.7, ...), custom_call_target="tpu_custom_call" | custom-call | tf_op jit(solution)/shard_map/segment_block/pallas_call | solution.py:492
  67.9 1.7 %copy.15 = bf16[320,320]{1,0:T(8,128)(2,1)} copy(bf16[320,320]{1,0:T(8,128)(2,1)} %segment_block.1) | data formatting | bytes 409600
